TPU v7x, 256 devices: a whole 4x4x8 slice. The times are simulated.
256 devices in a mesh: grp: 8 (over y, core), dev: 32 (over z, x).
Axes of the slice: x: 4, y: 4, z: 8, core: 2. Of those that a mesh axis runs over, the one named last changes fastest.
Arguments:
- node_feat: bfloat16 [1048576, 256], P(('grp', 'dev')), may hold values from -6 to 6
- coarse_feat: bfloat16 [131072, 256], P(('grp', 'dev')), may hold values from -6 to 6
- cotangent: bfloat16 [1048576, 256], P(('grp', 'dev')), may hold values from -6 to 6
- w_restrict: bfloat16 [256, 256], replicated, may hold values from -0.375 to 0.375
- w_coarse: bfloat16 [256, 256], replicated, may hold values from -0.375 to 0.375
- w_prolong: bfloat16 [256, 256], replicated, may hold values from -0.375 to 0.375
- owner: int32 [1048576], P(('grp', 'dev')), may hold values from 0 to 31, as said below
- slot: int32 [1048576], P(('grp', 'dev')), may hold values from 0 to 255
- recv_row: int32 [2097152], P(('grp', 'dev')), may hold values from 0 to 511
Outputs:
- grad_node: bfloat16 [1048576, 256], P(('grp', 'dev'))
- grad_coarse: bfloat16 [131072, 256], P(('grp', 'dev'))
- grad_wr: float32 [256, 256], replicated
- grad_wc: float32 [256, 256], replicated
- grad_wp: float32 [256, 256], replicated
Inputs may be any that keep to these rules, and one draw needn't show every extreme that they name: On each device the pairs (owner, slot) of its fine nodes are distinct, and exactly 256 of its fine nodes name the device's own index along dev.
All inputs are finite; a program needn't handle non-finite values.
Results may differ from a plain program's by a relative error of at most 0.01.
Values may be sent and summed in bfloat16 or wider, within the bound.
A program may use at most 128 MiB of HBM per device.

v0:
```python
import jax
import jax.numpy as jnp
from jax import lax
from jax.sharding import PartitionSpec as P


def dsilu(value):
    sig = jax.nn.sigmoid(value)
    return sig * (1.0 + value * (1.0 - sig))


def right_dot(left, right):
    return lax.dot_general(
        left, right, (((1,), (1,)), ((), ())), preferred_element_type=jnp.float32
    )


def left_dot(left, right):
    return lax.dot_general(
        left, right, (((0,), (0,)), ((), ())), preferred_element_type=jnp.float32
    )


def local(
    node_feat, coarse_feat, cotangent, w_restrict, w_coarse, w_prolong, owner, slot, recv_row
):
    peers = lax.axis_size("dev")
    block = recv_row.shape[0] // peers
    coarse_rows = coarse_feat.shape[0]
    width = node_feat.shape[1]
    flat_slot = owner * block + slot
    pre = jnp.dot(node_feat, w_restrict, preferred_element_type=jnp.float32)
    message = jax.nn.silu(pre).astype(jnp.bfloat16)
    outgoing = jnp.zeros((peers * block, width), jnp.bfloat16).at[flat_slot].set(message)
    incoming = lax.all_to_all(
        outgoing.reshape(peers, block, width), "dev", split_axis=0, concat_axis=0, tiled=True
    )
    member = (
        lax.broadcasted_iota(jnp.int32, (coarse_rows, peers * block), 0) == recv_row[None, :]
    ).astype(jnp.bfloat16)
    summed = coarse_feat.astype(jnp.float32) + jnp.dot(
        member, incoming.reshape(peers * block, width), preferred_element_type=jnp.float32
    )
    summed_b = summed.astype(jnp.bfloat16)
    update = jnp.dot(summed_b, w_coarse, preferred_element_type=jnp.float32)
    coarse_out = (summed + jax.nn.silu(update)).astype(jnp.bfloat16)
    returned = lax.all_to_all(
        coarse_out[recv_row].reshape(peers, block, width),
        "dev",
        split_axis=0,
        concat_axis=0,
        tiled=True,
    )
    parent_val = returned.reshape(peers * block, width)[flat_slot]
    proj = jnp.dot(parent_val, w_prolong, preferred_element_type=jnp.float32)
    grad_proj = (cotangent.astype(jnp.float32) * dsilu(proj)).astype(jnp.bfloat16)
    part_wp = left_dot(parent_val, grad_proj)
    term = right_dot(grad_proj, w_prolong).astype(jnp.bfloat16)
    outgoing_grad = jnp.zeros((peers * block, width), jnp.bfloat16).at[flat_slot].set(term)
    incoming_grad = lax.all_to_all(
        outgoing_grad.reshape(peers, block, width), "dev", split_axis=0, concat_axis=0, tiled=True
    )
    grad_out = jnp.dot(
        member, incoming_grad.reshape(peers * block, width), preferred_element_type=jnp.float32
    )
    grad_update = (grad_out * dsilu(update)).astype(jnp.bfloat16)
    grad_coarse = (grad_out + right_dot(grad_update, w_coarse)).astype(jnp.bfloat16)
    part_wc = left_dot(summed_b, grad_update)
    returned_grad = lax.all_to_all(
        grad_coarse[recv_row].reshape(peers, block, width),
        "dev",
        split_axis=0,
        concat_axis=0,
        tiled=True,
    )
    parent_grad = returned_grad.reshape(peers * block, width)[flat_slot]
    grad_pre = (parent_grad.astype(jnp.float32) * dsilu(pre)).astype(jnp.bfloat16)
    part_wr = left_dot(node_feat, grad_pre)
    grad_node = (cotangent.astype(jnp.float32) + right_dot(grad_pre, w_restrict)).astype(
        jnp.bfloat16
    )
    total_wr, total_wc, total_wp = lax.psum((part_wr, part_wc, part_wp), ("grp", "dev"))
    scale = float(node_feat.shape[0] * peers * lax.axis_size("grp")) ** (-0.5)
    return (grad_node, grad_coarse, total_wr * scale, total_wc * scale, total_wp * scale)


def solution(mesh):
    return jax.shard_map(
        local,
        mesh=mesh,
        in_specs=(
            P(("grp", "dev"), None),
            P(("grp", "dev"), None),
            P(("grp", "dev"), None),
            P(),
            P(),
            P(),
            P(("grp", "dev")),
            P(("grp", "dev")),
            P(("grp", "dev")),
        ),
        out_specs=(P(("grp", "dev"), None), P(("grp", "dev"), None), P(), P(), P()),
        check_vma=False,
    )
```

profile of v0, /device:TPU:1, one launch (start us, length us, event | category | flops | bytes accessed | tf_op | source)
XLA Modules:
  0.0 854.8 jit_solution(2394865283903365757)
XLA Ops:
  8.8 3.6 fusion.18
  12.4 21.8 %scatter_custom_fusion = bf16[8192,256]{1,0:T(8,128)(2,1)} fusion(s32[4096]{0:T(1024)S(1)} %get-tuple-element.14, f32[4096,256]{1,0:T(8,128)} %fusion.18, f32[]{:T(128)} %constant.11.clone.1, bf16[]{:T(256)} %constant.7.clone.1), kind=kCustom, calls=%fused_computation.19 | custom fusion | flops 5242880 | bytes 8388614 | tf_op jit(solution)/shard_map/scatter | solution.py:34
  34.2 12.1 %all-to-all-start = ((bf16[32,256,256]{2,1,0:T(8,128)(2,1)}), bf16[32,256,256]{2,1,0:T(8,128)(2,1)}, u32[]{:S(2)}, u32[]{:S(2)}) async-start(bf16[32,256,256]{2,1,0:T(8,128)(2,1)} %bitcast.29), calls=%async_computation | async-start | bytes 8388608 | tf_op jit(solution)/shard_map/all_to_all | solution.py:35
  46.4 93.0 %all-to-all-done = bf16[32,256,256]{2,1,0:T(8,128)(2,1)} async-done(((bf16[32,256,256]{2,1,0:T(8,128)(2,1)}), bf16[32,256,256]{2,1,0:T(8,128)(2,1)}, u32[]{:S(2)}, u32[]{:S(2)}) %all-to-all-start) | async-done | bytes 4194336 | tf_op jit(solution)/shard_map/all_to_all | solution.py:35
  139.4 4.8 fusion.11
  145.2 33.1 %gather_fusion = bf16[8192,256]{1,0:T(8,128)(2,1)} fusion(bf16[512,256]{1,0:T(8,128)(2,1)S(1)} %get-tuple-element.15, s32[8192]{0:T(1024)S(1)} %fusion.17), kind=kCustom, calls=%fused_computation | custom fusion | bytes 8421376 | tf_op jit(solution)/shard_map/gather | solution.py:48
  178.3 102.0 %all_to_all.20 = bf16[32,256,256]{2,1,0:T(8,128)(2,1)} all-to-all(bf16[32,256,256]{2,1,0:T(8,128)(2,1)} %bitcast.32), channel_id=1, replica_groups=mesh['grp'=8,'dev'=32] {'dev'}, dimensions={0} | all-to-all | bytes 8388608 | tf_op jit(solution)/shard_map/all_to_all | solution.py:47
  280.3 18.7 %gather_fusion.1 = bf16[4096,256]{1,0:T(8,128)(2,1)} fusion(bf16[8192,256]{1,0:T(8,128)(2,1)} %bitcast.28, s32[4096]{0:T(1024)S(1)} %get-tuple-element.13), kind=kCustom, calls=%fused_computation.1 | custom fusion | bytes 4210688 | tf_op jit(solution)/shard_map/gather | solution.py:54
  299.0 4.0 fusion.5
  303.1 1.3 copy-done.3
  304.4 2.1 convolution_convert_fusion
  306.5 20.9 %scatter_custom_fusion.1 = bf16[8192,256]{1,0:T(8,128)(2,1)} fusion(s32[4096]{0:T(1024)S(1)} %get-tuple-element.14, bf16[4096,256]{1,0:T(8,128)(2,1)} %convolution_convert_fusion, bf16[]{:T(256)} %constant.7.clone.1), kind=kCustom, calls=%fused_computation.21 | custom fusion | bytes 4194816 | tf_op jit(solution)/shard_map/scatter | solution.py:59
  327.4 99.7 %all_to_all.21 = bf16[32,256,256]{2,1,0:T(8,128)(2,1)S(1)} all-to-all(bf16[32,256,256]{2,1,0:T(8,128)(2,1)} %bitcast.30), channel_id=1, replica_groups=mesh['grp'=8,'dev'=32] {'dev'}, dimensions={0} | all-to-all | bytes 8388608 | tf_op jit(solution)/shard_map/all_to_all | solution.py:60
  427.2 2.6 fusion
  430.9 33.1 %gather_fusion.2 = bf16[8192,256]{1,0:T(8,128)(2,1)} fusion(bf16[512,256]{1,0:T(8,128)(2,1)S(1)} %fusion.12, s32[8192]{0:T(1024)S(1)} %fusion.17), kind=kCustom, calls=%fused_computation.2 | custom fusion | bytes 8421376 | tf_op jit(solution)/shard_map/gather | solution.py:70
  464.0 6.8 all-to-all-start.3
  471.1 3.9 fusion.19
  476.2 87.3 %all-to-all-done.3 = bf16[32,256,256]{2,1,0:T(8,128)(2,1)} async-done(((bf16[32,256,256]{2,1,0:T(8,128)(2,1)}), bf16[32,256,256]{2,1,0:T(8,128)(2,1)}, u32[]{:S(2)}, u32[]{:S(2)}) %all-to-all-start.3) | async-done | bytes 4194336 | tf_op jit(solution)/shard_map/all_to_all | solution.py:69
  563.5 18.7 %gather_fusion.3 = bf16[4096,256]{1,0:T(8,128)(2,1)} fusion(bf16[8192,256]{1,0:T(8,128)(2,1)} %bitcast.7, s32[4096]{0:T(1024)S(1)} %get-tuple-element.13), kind=kCustom, calls=%fused_computation.3 | custom fusion | bytes 4210688 | tf_op jit(solution)/shard_map/gather | solution.py:76
  582.1 4.4 multiply_convert_fusion
  586.6 1.3 copy-done.2
  587.9 1.5 convolution_bitcast_fusion
  589.4 4.3 fusion.4
  593.7 249.7 %all-reduce.3.cloned.1.call-done = (f32[256,256]{0,1:T(8,128)}, f32[256,256]{0,1:T(8,128)}, f32[256,256]{0,1:T(8,128)}) async-done(((f32[256,256]{0,1:T(8,128)}, f32[256,256]{0,1:T(8,128)}, f32[256,256]{0,1:T(8,128)}), (f32[256,256]{0,1:T(8,128)}, f32[256,256]{0,1:T(8,128)}, f32[256,256]{0,1:T(8,128)})) %all-reduce.3.cloned.1.call-update) | async-done | bytes 786448 | tf_op jit(solution)/shard_map/psum | solution.py:82
  (36 shorter events, 9.8 us)
Async XLA Ops:
  7.2 1.6 copy-start
  34.2 12.1 %copy-start.6 = (s32[8192]{0:T(1024)S(1)}, s32[8192]{0:T(1024)}, u32[]{:S(2)}) copy-start(s32[8192]{0:T(1024)} %param.17) | copy-start | bytes 98308
  34.2 105.2 %copy-start.7 = (bf16[512,256]{1,0:T(8,128)(2,1)S(1)}, bf16[512,256]{1,0:T(8,128)(2,1)}, u32[]{:S(2)}) copy-start(bf16[512,256]{1,0:T(8,128)(2,1)} %param.10) | copy-start | bytes 786436
  34.2 105.2 %all-to-all-start = ((bf16[32,256,256]{2,1,0:T(8,128)(2,1)}), bf16[32,256,256]{2,1,0:T(8,128)(2,1)}, u32[]{:S(2)}, u32[]{:S(2)}) async-start(bf16[32,256,256]{2,1,0:T(8,128)(2,1)} %bitcast.29), calls=%async_computation | async-start | bytes 8388608 | tf_op jit(solution)/shard_map/all_to_all | solution.py:35
  139.4 4.8 copy-start.8
  280.3 18.7 %copy-start.5 = (bf16[256,256]{1,0:T(8,128)(2,1)S(1)}, bf16[256,256]{1,0:T(8,128)(2,1)}, u32[]{:S(2)}) copy-start(bf16[256,256]{1,0:T(8,128)(2,1)} %param.14) | copy-start | bytes 393220
  303.1 1.3 copy-start.3
  427.2 3.4 copy-start.9
  429.7 0.8 copy-start.11
  430.9 33.1 %copy-start.1 = (bf16[512,256]{1,0:T(8,128)(2,1)}, bf16[512,256]{1,0:T(8,128)(2,1)S(1)}, u32[]{:S(2)}) copy-start(bf16[512,256]{1,0:T(8,128)(2,1)S(1)} %fusion.12) | copy-start | bytes 786436
  464.0 99.5 %all-to-all-start.3 = ((bf16[32,256,256]{2,1,0:T(8,128)(2,1)}), bf16[32,256,256]{2,1,0:T(8,128)(2,1)}, u32[]{:S(2)}, u32[]{:S(2)}) async-start(bf16[32,256,256]{2,1,0:T(8,128)(2,1)} %bitcast.31), calls=%async_computation.3 | async-start | bytes 8388608 | tf_op jit(solution)/shard_map/all_to_all | solution.py:69
  470.8 372.5 %all-reduce.3.cloned.1.call-start = ((), (), s32[]{:S(2)}) async-start(), calls=%async_computation.4 | async-start | bytes 1572864 | tf_op jit(solution)/shard_map/psum | solution.py:82
  471.1 4.0 copy-start.10
  471.1 4.0 copy-start.12
  586.6 1.3 copy-start.2
  587.9 1.5 copy-start.4
Sparse Core Ops, SparseCore 0:
  589.5 253.8 all-reduce.2
where the time goes:
time: 856 us; the launch traced here: 855 us
  waiting for transfers between devices  430 us (50%)
  blocking collectives  202 us (24%)
  local copies, waits for them, and re-layouts  131 us (15%)
  other arithmetic  29.2 us (3%)
  matrix products  29.2 us (3%)
  starting transfers between devices  19.2 us (2%)
  between operations  14.2 us (2%)
    psum x1, waiting for transfers between devices, local(): lax.psum((part_wr, part_wc, part_wp), ('grp', 'dev'))  250 us
    all_to_all x1, blocking collectives, local(): lax.all_to_all(coarse_out[recv_row].reshape(peers, block, width), 'dev',...  102 us
    all_to_all x1, blocking collectives, local(): lax.all_to_all(outgoing_grad.reshape(peers, block, width), 'dev', split_a...  99.7 us
    all_to_all x1, waiting for transfers between devices, local(): lax.all_to_all(outgoing.reshape(peers, block, width), 'dev', split_axis=0...  93 us
    all_to_all x1, waiting for transfers between devices, local(): lax.all_to_all(grad_coarse[recv_row].reshape(peers, block, width), 'dev',...  87.3 us
    gather x1, local copies, waits for them, and re-layouts, local(): coarse_out[recv_row].reshape(peers, block, width)  33.1 us
    gather x1, local copies, waits for them, and re-layouts, local(): grad_coarse[recv_row].reshape(peers, block, width)  33.1 us
    scatter x1, other arithmetic, local(): jnp.zeros((peers * block, width), jnp.bfloat16).at[flat_slot].set(message)  21.8 us
  transfers between devices with their start and end apart: 3, of which 3 were waited for; matrix products, arithmetic and copies ran while one was open for 1% of the time, Pallas kernels for 0%

commit v1 on v0

v1 whole, which is shorter than its diff:
```python
import functools

import jax
import jax.numpy as jnp
from jax import lax
from jax.experimental import pallas as pl
from jax.experimental.pallas import tpu as pltpu
from jax.sharding import PartitionSpec as P

ZN, XN = 8, 4
MESH = pl.DeviceIdType.MESH


def dsilu(value):
    sig = jax.nn.sigmoid(value)
    return sig * (1.0 + value * (1.0 - sig))


def dot(left, right):
    return jnp.dot(left, right, preferred_element_type=jnp.float32)


def right_dot(left, right):
    return lax.dot_general(
        left, right, (((1,), (1,)), ((), ())), preferred_element_type=jnp.float32
    )


def left_dot(left, right):
    return lax.dot_general(
        left, right, (((0,), (0,)), ((), ())), preferred_element_type=jnp.float32
    )


def hot(same):
    one = jnp.ones(same.shape, jnp.bfloat16)
    return jnp.where(same, one, jnp.zeros_like(one))


def rows_hot(keys, first, count):
    shape = (count, keys.shape[1])
    at = lax.broadcasted_iota(jnp.int32, shape, 0).astype(jnp.int16)
    return hot(at == jnp.broadcast_to((keys - first).astype(jnp.int16), shape))


def columns_hot(keys, count):
    lanes = keys.shape[1]
    at = lax.broadcasted_iota(jnp.int32, keys.shape, 1)
    parts = [hot((at + lane).astype(jnp.int16) == keys) for lane in range(0, count, lanes)]
    return jnp.concatenate(parts, axis=1)


def turned(keys):
    return jnp.transpose(jnp.broadcast_to(keys, (128, keys.shape[1])))


def sum_off(t):
    return lax.div(8 - t, 2) * (2 * lax.rem(t, 2) - 1)


def cast_off(t):
    return lax.div(t + 1, 2) * (2 * lax.rem(t, 2) - 1)


def remote(src, dst, send_sem, recv_sem, to):
    return pltpu.make_async_remote_copy(
        src_ref=src,
        dst_ref=dst,
        send_sem=send_sem,
        recv_sem=recv_sem,
        device_id=to,
        device_id_type=MESH,
    )


class Here:
    def __init__(self):
        dev = lax.axis_index("dev")
        self.g = lax.axis_index("grp")
        self.z, self.x = lax.div(dev, XN), lax.rem(dev, XN)

    def plane(self, off):
        return lax.rem(self.z + off + ZN, ZN)

    def at_z(self, off):
        return {"dev": self.plane(off) * XN + self.x}

    def at_x(self, x):
        return {"dev": self.z * XN + x}

    def greet(self, groups):
        barrier = pltpu.get_barrier_semaphore()
        partners = [self.at_z(i) for i in range(1, ZN)]
        partners += [self.at_x(lax.rem(self.x + i, XN)) for i in range(1, XN)]
        partners += [{"grp": lax.rem(self.g + i, groups)} for i in range(1, groups)]
        for partner in partners:
            pl.semaphore_signal(barrier, inc=1, device_id=partner, device_id_type=MESH)
        pl.semaphore_wait(barrier, len(partners))


class Rows:
    def __init__(self, here, out, into, pass_r, pass_l, send_sem, recv_sem):
        self.here = here
        self.out, self.into = out, into
        self.passing = pass_r, pass_l
        self.sems = send_sem, recv_sem
        self.block = out.shape[1] // XN

    def copy(self, i, u):
        x, block = self.here.x, self.block
        half = block // 2
        right, left, far = lax.rem(x + 1, XN), lax.rem(x + 3, XN), lax.rem(x + 2, XN)

        def part(ref, at, first, count):
            return ref.at[u, pl.ds(pl.multiple_of(at * block + first, half), count)]

        pass_r, pass_l = self.passing
        if i == 0:
            src, dst, to = part(self.out, far, 0, half), pass_r.at[u], right
        elif i == 1:
            src, dst, to = part(self.out, far, half, half), pass_l.at[u], left
        elif i == 2:
            src, dst, to = part(self.out, right, 0, block), part(self.into, x, 0, block), right
        elif i == 3:
            src, dst, to = part(self.out, left, 0, block), part(self.into, x, 0, block), left
        elif i == 4:
            src, dst, to = pass_r.at[u], part(self.into, left, 0, half), right
        else:
            src, dst, to = pass_l.at[u], part(self.into, right, half, half), left
        return remote(src, dst, self.sems[0].at[i, u], self.sems[1].at[i, u], self.here.at_x(to))

    def start(self, u):
        own = pl.ds(pl.multiple_of(self.here.x * self.block, self.block), self.block)
        for i in range(4):
            self.copy(i, u).start()
        self.into[u, own, :] = self.out[u, own, :]

    def pass_on(self, u):
        for i in (0, 1):
            self.copy(i, u).wait_recv()
            self.copy(i + 4, u).start()

    def arrived(self, u):
        for i in range(2, 6):
            self.copy(i, u).wait_recv()

    def close(self):
        @pl.loop(0, ZN)
        def _(u):
            for i in range(6):
                self.copy(i, u).wait_send()


def sum_to_owners(here, rows, produce, keys, finish, out_z, got, z_send, z_recv):
    half = out_z.shape[1] // 2
    low, high = pl.ds(0, half), pl.ds(half, half)

    def z_copy(t):
        return remote(
            out_z.at[t], got.at[t + 2], z_send.at[t], z_recv.at[t + 2], here.at_z(2 * lax.rem(t, 2) - 1)
        )

    def first_up():
        return remote(out_z.at[0, low], got.at[1, low], z_send.at[0], z_recv.at[1], here.at_z(1))

    def first_down():
        return remote(out_z.at[0, high], got.at[2, high], z_send.at[7], z_recv.at[2], here.at_z(-1))

    def gather_up(t):
        u = here.plane(sum_off(t))
        rows.arrived(u)
        pl.when(t == 1)(lambda: first_up().wait_recv())
        pl.when(t == 2)(lambda: first_down().wait_recv())
        pl.when(t >= 3)(lambda: z_copy(t - 2).wait_recv())
        pl.when(t == ZN - 1)(lambda: z_copy(t - 1).wait_recv())

        @pl.loop(0, 2)
        def _(part):
            first = pl.multiple_of(part * half, half)
            span = pl.ds(first, half)
            total = dot(rows_hot(keys[u], first, half), rows.into[u])
            total = total + got[t, span, :].astype(jnp.float32)

            @pl.when(t == ZN - 1)
            def _():
                finish(span, total + got[ZN, span, :].astype(jnp.float32))

            @pl.when(t < ZN - 1)
            def _():
                out_z[t, span, :] = total.astype(jnp.bfloat16)

        @pl.when(t == 0)
        def _():
            first_up().start()
            first_down().start()

        @pl.when((t > 0) & (t < ZN - 1))
        def _():
            z_copy(t).start()

    @pl.loop(0, ZN + 2)
    def _(i):
        @pl.when(i < ZN)
        def _():
            u = here.plane(sum_off(i))
            produce(i, u)
            rows.start(u)

        @pl.when((i >= 1) & (i <= ZN))
        def _():
            rows.pass_on(here.plane(sum_off(i - 1)))

        @pl.when(i >= 2)
        def _():
            gather_up(i - 2)

    rows.close()
    first_up().wait_send()
    first_down().wait_send()

    @pl.loop(1, ZN - 1)
    def _(t):
        z_copy(t).wait_send()


def cast_to_children(here, rows, keys, prepare, consume, chunks, z_send, z_recv):
    half = chunks.shape[1] // 2
    low, high = pl.ds(0, half), pl.ds(half, half)
    count = rows.out.shape[1] // 2

    def z_copy(t):
        return remote(
            chunks.at[t], chunks.at[t + 2], z_send.at[t], z_recv.at[t + 2], here.at_z(1 - 2 * lax.rem(t, 2))
        )

    def first_down():
        return remote(chunks.at[0], chunks.at[1], z_send.at[0], z_recv.at[1], here.at_z(-1))

    def first_up():
        return remote(chunks.at[0], chunks.at[2], z_send.at[7], z_recv.at[2], here.at_z(1))

    def last_down():
        return remote(chunks.at[5, high], chunks.at[7, high], z_send.at[5], z_recv.at[7], here.at_z(-1))

    def last_up():
        return remote(chunks.at[6, low], chunks.at[7, low], z_send.at[6], z_recv.at[8], here.at_z(1))

    def spread(t, u):
        pl.when(t == 1)(lambda: first_down().wait_recv())
        pl.when(t == 2)(lambda: first_up().wait_recv())
        pl.when((t >= 3) & (t < ZN - 1))(lambda: z_copy(t - 2).wait_recv())

        @pl.when(t == 0)
        def _():
            first_down().start()
            first_up().start()

        pl.when((t > 0) & (t < 5))(lambda: z_copy(t).start())
        pl.when(t == 5)(lambda: last_down().start())
        pl.when(t == 6)(lambda: last_up().start())

        @pl.when(t == ZN - 1)
        def _():
            last_down().wait_recv()
            last_up().wait_recv()

        wanted = keys[u]
        for part in range(2):
            span = pl.ds(part * count, count)
            chosen = columns_hot(
                turned(wanted[:, part * count:(part + 1) * count]).astype(jnp.int16), chunks.shape[1]
            )
            rows.out[u, span, :] = dot(chosen, chunks[t]).astype(jnp.bfloat16)

    @pl.loop(0, ZN + 2)
    def _(i):
        @pl.when(i < ZN)
        def _():
            u = here.plane(cast_off(i))
            spread(i, u)
            rows.start(u)

        @pl.when((i >= 1) & (i <= ZN))
        def _():
            rows.pass_on(here.plane(cast_off(i - 1)))

        prepare(i)

        @pl.when(i >= 2)
        def _():
            u = here.plane(cast_off(i - 2))
            rows.arrived(u)
            consume(i - 2, u)

    rows.close()
    for copy in (first_down, first_up, last_down, last_up):
        copy().wait_send()

    @pl.loop(1, 5)
    def _(t):
        z_copy(t).wait_send()


def to_slots(slots, values, first, count):
    nodes = values.shape[0]
    step = min(1024, nodes)
    total = jnp.zeros((count, values.shape[1]), jnp.float32)
    for at in range(0, nodes, step):
        total = total + dot(rows_hot(slots[:, at:at + step], first, count), values[at:at + step, :])
    return total.astype(jnp.bfloat16)


class Total:
    def __init__(self, here, part, scale, by_g, mid, by_x, one, by_z, done, full_x, full, sems):
        self.here, self.part, self.scale = here, part, scale
        self.by_g, self.mid, self.by_x, self.one = by_g, mid, by_x, one
        self.by_z, self.done, self.full_x, self.full = by_z, done, full_x, full
        self.sems = sems
        self.groups = part.shape[1]

    def peers(self, stage):
        here, groups = self.here, self.groups
        if stage in (0, 4):
            return [lax.rem(here.g + i, groups) for i in range(1, groups)]
        if stage == 2:
            return [here.plane(i) for i in range(1, ZN)]
        return [lax.rem(here.x + i, XN) for i in range(1, XN)]

    def copy(self, stage, i, peer):
        here = self.here
        send, recv = self.sems.at[0, stage, i], self.sems.at[1, stage, i]
        if stage == 0:
            return remote(self.part.at[:, peer], self.by_g.at[:, here.g], send, recv, {"grp": peer})
        if stage == 1:
            return remote(self.mid.at[:, peer], self.by_x.at[:, here.x], send, recv, here.at_x(peer))
        if stage == 2:
            return remote(self.one, self.by_z.at[here.z], send, recv, {"dev": peer * XN + here.x})
        if stage == 3:
            return remote(self.done, self.full_x.at[:, here.x], send, recv, here.at_x(peer))
        return remote(self.full_x, self.full.at[:, here.g], send, recv, {"grp": peer})

    def start(self, stage):
        here = self.here
        for i, peer in enumerate(self.peers(stage)):
            self.copy(stage, i, peer).start()
        if stage == 0:
            self.by_g[:, here.g] = self.part[:, here.g]
        elif stage == 1:
            self.by_x[:, here.x] = self.mid[:, here.x]
        elif stage == 2:
            self.by_z[here.z] = self.one[...]
        elif stage == 3:
            self.full_x[:, here.x] = self.done[...]
        else:
            self.full[:, here.g] = self.full_x[...]

    def end(self, stage):
        for i, peer in enumerate(self.peers(stage)):
            self.copy(stage, i, peer).wait()
        if stage == 0:
            self.mid[...] = jnp.sum(self.by_g[...], axis=1).reshape(self.mid.shape)
        elif stage == 1:
            self.one[...] = jnp.sum(self.by_x[...], axis=1)
        elif stage == 2:
            self.done[...] = jnp.sum(self.by_z[...], axis=0) * self.scale

    def next(self, stage):
        if stage:
            self.end(stage - 1)
        if stage < 5:
            self.start(stage)


def block_kernel(
    scale,
    feat, cot, slots, recv_row, coarse, wr, wc, wp,
    grad_node, grad_coarse, totals,
    keys, feat_slot, cot_slot, out, term,
    summed_b, update, places, grad_pre, back,
    into_a, pass_ra, pass_la, into_b, pass_rb, pass_lb, out_z, got, chunks,
    x_send_a, x_recv_a, x_send_b, x_recv_b, z_send_a, z_recv_a, z_send_b, z_recv_b, k_send, k_recv,
    part_cp, part_r, *total_refs,
):
    here = Here()
    nodes = feat.shape[0]
    width = feat_slot.shape[1]
    count = width // 2
    step = min(512, nodes)
    half = coarse.shape[0] // 2
    groups = part_r.shape[1]
    kept = cot_slot.shape[0]

    got[0] = jnp.zeros_like(got[0])
    got[1, half:, :] = jnp.zeros_like(got[1, half:, :])
    got[2, :half, :] = jnp.zeros_like(got[2, :half, :])
    part_cp[...] = jnp.zeros_like(part_cp)
    part_r[...] = jnp.zeros_like(part_r)
    here.greet(groups)

    def key_copy(off):
        to = here.plane(off)
        return remote(
            recv_row.at[to], keys.at[here.z], k_send.at[off], k_recv.at[off], {"dev": to * XN + here.x}
        )

    for off in range(1, ZN):
        key_copy(off).start()
    keys[here.z] = recv_row[here.z]

    def add(ref, at, value):
        ref[at] += value.reshape(ref.shape[1:])

    def make_message(t, u):
        @pl.loop(0, 2)
        def _(part):
            span = pl.ds(pl.multiple_of(part * count, count), count)
            block = to_slots(slots, feat, u * width + part * count, count)
            feat_slot[u, span, :] = block
            pre = dot(block, wr[...])
            out[u, span, :] = (pre * jax.nn.sigmoid(pre)).astype(jnp.bfloat16)

        @pl.when(t == 1)
        def _():
            for off in range(1, ZN):
                key_copy(off).wait_recv()

    def coarse_update(span, total):
        summed = coarse[span, :].astype(jnp.float32) + total
        rounded = summed.astype(jnp.bfloat16)
        moved = dot(rounded, wc[...])
        summed_b[span, :] = rounded
        update[span, :] = moved
        chunks[0, span, :] = (summed + moved * jax.nn.sigmoid(moved)).astype(jnp.bfloat16)

    rows_a = Rows(here, out, into_a, pass_ra, pass_la, x_send_a, x_recv_a)
    sum_to_owners(here, rows_a, make_message, keys, coarse_update, out_z, got, z_send_a, z_recv_a)
    for off in range(1, ZN):
        key_copy(off).wait_send()

    def place_cotangent(i):
        @pl.when(i < ZN)
        def _():
            first = here.plane(cast_off(i)) * width
            spot = lax.rem(i, kept)

            @pl.loop(0, 2)
            def _(part):
                span = pl.ds(pl.multiple_of(part * count, count), count)
                cot_slot[spot, span, :] = to_slots(slots, cot, first + part * count, count)

    def make_term(t, u):
        spot = lax.rem(t, kept)

        @pl.loop(0, 2)
        def _(part):
            span = pl.ds(pl.multiple_of(part * count, count), count)
            parent = into_b[u, span, :]
            proj = dot(parent, wp[...])
            grad = (cot_slot[spot, span, :].astype(jnp.float32) * dsilu(proj)).astype(jnp.bfloat16)
            add(part_cp, 1, left_dot(parent, grad))
            term[u, span, :] = right_dot(grad, wp[...]).astype(jnp.bfloat16)

    rows_b = Rows(here, out, into_b, pass_rb, pass_lb, x_send_b, x_recv_b)
    cast_to_children(here, rows_b, keys, place_cotangent, make_term, chunks, z_send_b, z_recv_b)

    def coarse_gradient(span, total):
        grad_update = (total * dsilu(update[span, :])).astype(jnp.bfloat16)
        grad = (total + right_dot(grad_update, wc[...])).astype(jnp.bfloat16)
        grad_coarse[span, :] = grad
        chunks[0, span, :] = grad
        add(part_cp, 0, left_dot(summed_b[span, :], grad_update))

    rows_a = Rows(here, term, into_a, pass_ra, pass_la, x_send_a, x_recv_a)
    sum_to_owners(
        here, rows_a, lambda t, u: None, keys, coarse_gradient, out_z, got, z_send_a, z_recv_a
    )

    sums_cp = Total(here, part_cp, scale, *total_refs[:8], total_refs[16])
    sums_r = Total(here, part_r, scale, *total_refs[8:16], total_refs[17])

    def other_sums(i):
        for stage in range(6):
            pl.when(i == stage)(functools.partial(sums_cp.next, stage))

        @pl.when(i == 0)
        def _():
            back[...] = jnp.zeros_like(back)
            for at in range(0, nodes, step):
                places[at:at + step, :] = turned(slots[:, at:at + step])

    def node_gradient(t, u):
        @pl.loop(0, 2)
        def _(part):
            span = pl.ds(pl.multiple_of(part * count, count), count)
            block = feat_slot[u, span, :]
            pre = dot(block, wr[...])
            grad = (into_b[u, span, :].astype(jnp.float32) * dsilu(pre)).astype(jnp.bfloat16)
            add(part_r, 0, left_dot(block, grad))
            grad_pre[span, :] = grad

        pl.when(t == ZN - 1)(functools.partial(sums_r.next, 0))
        first = u * width

        @pl.loop(0, nodes // step)
        def _(part):
            span = pl.ds(pl.multiple_of(part * step, step), step)
            wanted = (places[span, :] - first).astype(jnp.int16)
            found = dot(columns_hot(wanted, width), grad_pre[...])
            back[span, :] = (back[span, :].astype(jnp.float32) + found).astype(jnp.bfloat16)

    rows_b = Rows(here, out, into_b, pass_rb, pass_lb, x_send_b, x_recv_b)
    cast_to_children(here, rows_b, keys, other_sums, node_gradient, chunks, z_send_b, z_recv_b)
    sums_r.next(1)

    @pl.loop(0, nodes // step)
    def _(part):
        span = pl.ds(pl.multiple_of(part * step, step), step)
        grad_node[span, :] = (
            cot[span, :].astype(jnp.float32) + right_dot(back[span, :], wr[...])
        ).astype(jnp.bfloat16)

    for stage in range(2, 6):
        sums_r.next(stage)
    totals[0] = sums_r.full[0].reshape(totals.shape[1:])
    for at in (0, 1):
        totals[at + 1] = sums_cp.full[at].reshape(totals.shape[1:])


def total_scratch(m, groups, width):
    rows = width // groups
    part = rows // XN
    return [
        pltpu.VMEM((m, groups, rows, width), jnp.float32),
        pltpu.VMEM((m, XN, part, width), jnp.float32),
        pltpu.VMEM((m, XN, part, width), jnp.float32),
        pltpu.VMEM((m, part, width), jnp.float32),
        pltpu.VMEM((ZN, m, part, width), jnp.float32),
        pltpu.VMEM((m, part, width), jnp.float32),
        pltpu.VMEM((m, XN, part, width), jnp.float32),
        pltpu.VMEM((m, groups, XN, part, width), jnp.float32),
    ]


def local(
    node_feat, coarse_feat, cotangent, w_restrict, w_coarse, w_prolong, owner, slot, recv_row
):
    devs = ZN * XN
    groups = lax.axis_size("grp")
    nodes, width = node_feat.shape
    coarse_rows = coarse_feat.shape[0]
    block = recv_row.shape[0] // devs
    plane_rows = XN * block
    bf, f32 = jnp.bfloat16, jnp.float32
    shape = jax.ShapeDtypeStruct
    dma = pltpu.SemaphoreType.DMA
    vmem = pltpu.VMEM
    wide = vmem((ZN, plane_rows, width), bf)
    passing = vmem((ZN, block // 2, width), bf)
    scratch = [
        vmem((ZN, 1, plane_rows), jnp.int32),
        wide,
        vmem((4, plane_rows, width), bf),
        wide,
        wide,
        vmem((coarse_rows, width), bf),
        vmem((coarse_rows, width), f32),
        vmem((nodes, 128), jnp.int32),
        vmem((plane_rows, width), bf),
        vmem((nodes, width), bf),
        wide, passing, passing,
        wide, passing, passing,
        vmem((ZN, coarse_rows, width), bf),
        vmem((ZN + 1, coarse_rows, width), bf),
        vmem((ZN, coarse_rows, width), bf),
    ]
    scratch += [dma((6, ZN))] * 4 + [dma((ZN,)), dma((ZN + 1,))] * 2 + [dma((ZN,))] * 2
    scratch += [
        vmem((2, groups, width // groups, width), f32),
        vmem((1, groups, width // groups, width), f32),
    ]
    scratch += total_scratch(2, groups, width) + total_scratch(1, groups, width)
    scratch += [dma((2, 5, ZN))] * 2
    in_vmem = pl.BlockSpec(memory_space=pltpu.VMEM)
    scale = float(nodes * devs * groups) ** (-0.5)
    grad_node, grad_coarse, totals = pl.pallas_call(
        functools.partial(block_kernel, scale),
        out_shape=(
            shape((nodes, width), bf),
            shape((coarse_rows, width), bf),
            shape((3, width, width), f32),
        ),
        in_specs=[in_vmem] * 8,
        out_specs=(in_vmem,) * 3,
        scratch_shapes=scratch,
        compiler_params=pltpu.CompilerParams(
            collective_id=0, has_side_effects=True, vmem_limit_bytes=62 * 2**20
        ),
    )(
        node_feat, cotangent, (owner * block + slot).reshape(1, nodes),
        recv_row.reshape(ZN, 1, plane_rows), coarse_feat, w_restrict, w_coarse, w_prolong,
    )
    return grad_node, grad_coarse, totals[0], totals[1], totals[2]


def solution(mesh):
    return jax.shard_map(
        local,
        mesh=mesh,
        in_specs=(
            P(("grp", "dev"), None),
            P(("grp", "dev"), None),
            P(("grp", "dev"), None),
            P(),
            P(),
            P(),
            P(("grp", "dev")),
            P(("grp", "dev")),
            P(("grp", "dev")),
        ),
        out_specs=(P(("grp", "dev"), None), P(("grp", "dev"), None), P(), P(), P()),
        check_vma=False,
    )
```

time: 856 us -> 268 us (0.31)
  waiting for transfers between devices: 430 us -> 0 us
  Pallas kernels: 0 us -> 260 us
  blocking collectives: 202 us -> 0 us
  local copies, waits for them, and re-layouts: 131 us -> 5.8 us
  matrix products: 29.2 us -> 0 us
  other arithmetic: 29.2 us -> 1.34 us
  starting transfers between devices: 19.2 us -> 0 us
  between operations: 14.2 us -> 0.64 us
    pallas_call x0 -> x1, Pallas kernels: none -> 260 us  [local(): pl.pallas_call(functools.partial(block_kernel, scale), out_shape=(shape((...]
    psum x1 -> x0, waiting for transfers between devices: 250 us -> none  [local(): lax.psum((part_wr, part_wc, part_wp), ('grp', 'dev'))]
    all_to_all x2 -> x0, blocking collectives: 202 us -> none  [the longest x1 102 us: local(): lax.all_to_all(coarse_out[recv_row].reshape(peers, block, width), 'dev',...]
    all_to_all x2 -> x0, waiting for transfers between devices: 180 us -> none  [the longest x1 93 us: local(): lax.all_to_all(outgoing.reshape(peers, block, width), 'dev', split_axis=0...]
    gather x4 -> x0, local copies, waits for them, and re-layouts: 104 us -> none  [the longest x1 33.1 us: local(): coarse_out[recv_row].reshape(peers, block, width)]
    dot_general x11 -> x0, matrix products: 29.2 us -> none  [the longest x3 6.76 us: right_dot(): lax.dot_general(left, right, (((1,), (1,)), ((), ())), preferred_element_...]
    scatter x1 -> x0, other arithmetic: 21.8 us -> none  [local(): jnp.zeros((peers * block, width), jnp.bfloat16).at[flat_slot].set(message)]
    scatter x1 -> x0, local copies, waits for them, and re-layouts: 20.9 us -> none  [local(): jnp.zeros((peers * block, width), jnp.bfloat16).at[flat_slot].set(term)]
  transfers between devices with their start and end apart: 3 -> 0, of which waited for: 3 -> 0; matrix products, arithmetic and copies ran while one was open for 1% -> 0% of each run, Pallas kernels for 0% -> 0%
where the time goes in v1:
time: 268 us; the launch traced here: 267 us
  Pallas kernels  260 us (97%)
  local copies, waits for them, and re-layouts  5.8 us (2%)
    pallas_call x1, Pallas kernels, local(): pl.pallas_call(functools.partial(block_kernel, scale), out_shape=(shape((...  260 us

profile of v1, /device:TPU:1, one launch (start us, length us, event | category | flops | bytes accessed | tf_op | source)
XLA Modules:
  0.0 267.3 jit_solution(6252409267754430603)
XLA Ops:
  0.6 1.3 multiply_add_fusion
  2.0 259.5 %shard_map.128 = (bf16[4096,256]{1,0:T(8,128)(2,1)}, bf16[512,256]{1,0:T(8,128)(2,1)}, f32[3,256,256]{2,1,0:T(8,128)}) custom-call(bf16[4096,256]{1,0:T(8,128)(2,1)} %feat.1, bf16[4096,256]{1,0:T(8,128)(2,1)} %cot.1, s32[1,4096]{1,0:T(1,128)} %bitcast.8, s32[8,1,1024]{2,1,0:T(1,128)} %bitcast.9, bf16[512,256]{1,0:T(8,128)(2,1)} %coarse.1, ...), custom_call_target="tpu_custom_call" | custom-call | tf_op jit(solution)/shard_map/pallas_call | solution.py:585
  261.5 2.0 slice_bitcast_fusion
  263.5 0.0 copy-start
  263.5 3.1 %copy.16 = bf16[4096,256]{1,0:T(8,128)(2,1)} copy(bf16[4096,256]{1,0:T(8,128)(2,1)} %get-tuple-element.19) | data formatting | bytes 4194304
  266.6 0.0 copy-done
  266.6 0.7 copy.17
Async XLA Ops:
  263.5 3.1 %copy-start = (bf16[512,256]{1,0:T(8,128)(2,1)S(1)}, bf16[512,256]{1,0:T(8,128)(2,1)}, u32[]{:S(2)}) copy-start(bf16[512,256]{1,0:T(8,128)(2,1)} %get-tuple-element.20) | copy-start | bytes 786436

commit v2 on v1

v2 whole, which is shorter than its diff:
```python
import functools

import jax
import jax.numpy as jnp
from jax import lax
from jax.experimental import pallas as pl
from jax.experimental.pallas import tpu as pltpu
from jax.sharding import PartitionSpec as P

ZN, XN = 8, 4
MESH = pl.DeviceIdType.MESH


def dsilu(value):
    sig = jax.nn.sigmoid(value)
    return sig * (1.0 + value * (1.0 - sig))


def dot(left, right):
    return jnp.dot(left, right, preferred_element_type=jnp.float32)


def right_dot(left, right):
    return lax.dot_general(
        left, right, (((1,), (1,)), ((), ())), preferred_element_type=jnp.float32
    )


def left_dot(left, right):
    return lax.dot_general(
        left, right, (((0,), (0,)), ((), ())), preferred_element_type=jnp.float32
    )


def hot(same):
    one = jnp.ones(same.shape, jnp.bfloat16)
    return jnp.where(same, one, jnp.zeros_like(one))


def rows_hot(keys, first, count):
    shape = (count, keys.shape[1])
    at = lax.broadcasted_iota(jnp.int32, shape, 0).astype(jnp.int16)
    return hot(at == jnp.broadcast_to((keys - first).astype(jnp.int16), shape))


def columns_hot(keys, count):
    lanes = keys.shape[1]
    at = lax.broadcasted_iota(jnp.int32, keys.shape, 1)
    parts = [hot((at + lane).astype(jnp.int16) == keys) for lane in range(0, count, lanes)]
    return jnp.concatenate(parts, axis=1)


def turned(keys):
    return jnp.transpose(jnp.broadcast_to(keys, (128, keys.shape[1])))


def sum_off(t):
    return lax.div(8 - t, 2) * (2 * lax.rem(t, 2) - 1)


def cast_off(t):
    return lax.div(t + 1, 2) * (2 * lax.rem(t, 2) - 1)


def remote(src, dst, send_sem, recv_sem, to):
    return pltpu.make_async_remote_copy(
        src_ref=src,
        dst_ref=dst,
        send_sem=send_sem,
        recv_sem=recv_sem,
        device_id=to,
        device_id_type=MESH,
    )


class Here:
    def __init__(self):
        dev = lax.axis_index("dev")
        self.g = lax.axis_index("grp")
        self.z, self.x = lax.div(dev, XN), lax.rem(dev, XN)
        self.right, self.far, self.left = (lax.rem(self.x + i, XN) for i in (1, 2, 3))

    def plane(self, off):
        return lax.rem(self.z + off + ZN, ZN)

    def at_z(self, off):
        return {"dev": self.plane(off) * XN + self.x}

    def at_x(self, x):
        return {"dev": self.z * XN + x}

    def greet(self, groups):
        barrier = pltpu.get_barrier_semaphore()
        partners = [self.at_z(i) for i in range(1, ZN)]
        partners += [{"dev": self.plane(i) * XN + self.far} for i in range(ZN)]
        partners += [self.at_x(self.right), self.at_x(self.left)]
        partners += [{"grp": lax.rem(self.g + i, groups)} for i in range(1, groups)]
        for partner in partners:
            pl.semaphore_signal(barrier, inc=1, device_id=partner, device_id_type=MESH)
        pl.semaphore_wait(barrier, len(partners))


def block_at(x, block):
    return pl.ds(pl.multiple_of(x * block, block), block)


class Rows:
    def __init__(self, here, out, into, send_sem, recv_sem):
        self.here = here
        self.out, self.into = out, into
        self.sems = send_sem, recv_sem
        self.block = out.shape[1] // XN

    def copy(self, i, u):
        to = self.here.left if i else self.here.right
        return remote(
            self.out.at[u, block_at(to, self.block)],
            self.into.at[u, block_at(self.here.x, self.block)],
            self.sems[0].at[i, u],
            self.sems[1].at[i, u],
            self.here.at_x(to),
        )

    def start(self, u):
        own = block_at(self.here.x, self.block)
        for i in (0, 1):
            self.copy(i, u).start()
        self.into[u, own, :] = self.out[u, own, :]

    def arrived(self, u):
        for i in (0, 1):
            self.copy(i, u).wait_recv()

    def close(self):
        @pl.loop(0, ZN)
        def _(u):
            for i in (0, 1):
                self.copy(i, u).wait_send()


class Across:
    def __init__(self, here, src, dst, pass_r, pass_l, send_sem, recv_sem):
        self.here, self.src, self.dst = here, src, dst
        self.passing = pass_r, pass_l
        self.sems = send_sem, recv_sem
        self.half = src.shape[0] // 2

    def copy(self, i):
        span = pl.ds(i % 2 * self.half, self.half)
        buffer = self.passing[i % 2]
        src, dst = (self.src.at[span], buffer) if i < 2 else (buffer, self.dst.at[span])
        to = self.here.at_x(self.here.left if i % 2 else self.here.right)
        return remote(src, dst, self.sems[0].at[i], self.sems[1].at[i], to)

    def start(self):
        for i in (0, 1):
            self.copy(i).start()

    def pass_on(self):
        for i in (0, 1):
            self.copy(i).wait_recv()
            self.copy(i + 2).start()

    def arrived(self):
        for i in (2, 3):
            self.copy(i).wait_recv()

    def close(self):
        for i in range(4):
            self.copy(i).wait_send()


class SumChain:
    def __init__(self, here, out, got, send_sem, recv_sem):
        self.here, self.out, self.got = here, out, got
        self.send, self.recv = send_sem, recv_sem
        half = out.shape[1] // 2
        self.low, self.high = pl.ds(0, half), pl.ds(half, half)

    def copy(self, t):
        to = self.here.at_z(2 * lax.rem(t, 2) - 1)
        return remote(self.out.at[t], self.got.at[t + 2], self.send.at[t], self.recv.at[t + 2], to)

    def first_up(self):
        src, dst = self.out.at[0, self.low], self.got.at[1, self.low]
        return remote(src, dst, self.send.at[0], self.recv.at[1], self.here.at_z(1))

    def first_down(self):
        src, dst = self.out.at[0, self.high], self.got.at[2, self.high]
        return remote(src, dst, self.send.at[7], self.recv.at[2], self.here.at_z(-1))

    def clear(self):
        for at in (self.got.at[0], self.got.at[1, self.high], self.got.at[2, self.low]):
            at[...] = jnp.zeros(at.shape, at.dtype)

    def hold(self, t):
        pl.when(t == 1)(lambda: self.first_up().wait_recv())
        pl.when(t == 2)(lambda: self.first_down().wait_recv())
        pl.when(t >= 3)(lambda: self.copy(t - 2).wait_recv())
        pl.when(t == ZN - 1)(lambda: self.copy(t - 1).wait_recv())

    def start(self, t):
        @pl.when(t == 0)
        def _():
            self.first_up().start()
            self.first_down().start()

        pl.when((t > 0) & (t < ZN - 1))(lambda: self.copy(t).start())

    def close(self):
        self.first_up().wait_send()
        self.first_down().wait_send()

        @pl.loop(1, ZN - 1)
        def _(t):
            self.copy(t).wait_send()


class CastChain:
    def __init__(self, here, chunks, send_sem, recv_sem):
        self.here, self.chunks = here, chunks
        self.send, self.recv = send_sem, recv_sem
        half = chunks.shape[1] // 2
        self.low, self.high = pl.ds(0, half), pl.ds(half, half)

    def copy(self, t):
        to = self.here.at_z(1 - 2 * lax.rem(t, 2))
        return remote(self.chunks.at[t], self.chunks.at[t + 2], self.send.at[t], self.recv.at[t + 2], to)

    def first_down(self):
        src, dst = self.chunks.at[0], self.chunks.at[1]
        return remote(src, dst, self.send.at[0], self.recv.at[1], self.here.at_z(-1))

    def first_up(self):
        src, dst = self.chunks.at[0], self.chunks.at[2]
        return remote(src, dst, self.send.at[7], self.recv.at[2], self.here.at_z(1))

    def last_down(self):
        src, dst = self.chunks.at[5, self.high], self.chunks.at[7, self.high]
        return remote(src, dst, self.send.at[5], self.recv.at[7], self.here.at_z(-1))

    def last_up(self):
        src, dst = self.chunks.at[6, self.low], self.chunks.at[7, self.low]
        return remote(src, dst, self.send.at[6], self.recv.at[8], self.here.at_z(1))

    def step(self, t):
        pl.when(t == 1)(lambda: self.first_down().wait_recv())
        pl.when(t == 2)(lambda: self.first_up().wait_recv())
        pl.when((t >= 3) & (t < ZN - 1))(lambda: self.copy(t - 2).wait_recv())

        @pl.when(t == 0)
        def _():
            self.first_down().start()
            self.first_up().start()

        pl.when((t > 0) & (t < 5))(lambda: self.copy(t).start())
        pl.when(t == 5)(lambda: self.last_down().start())
        pl.when(t == 6)(lambda: self.last_up().start())

        @pl.when(t == ZN - 1)
        def _():
            self.last_down().wait_recv()
            self.last_up().wait_recv()

    def close(self):
        for copy in (self.first_down, self.first_up, self.last_down, self.last_up):
            copy().wait_send()

        @pl.loop(1, 5)
        def _(t):
            self.copy(t).wait_send()


def sum_to_owners(here, rows, near, far, across, produce, keys, far_keys, finish):
    half = near.out.shape[1] // 2

    def far_up(t, u):
        far.hold(t)
        values = rows.out[u, block_at(here.far, rows.block), :]

        @pl.loop(0, 2)
        def _(part):
            first = pl.multiple_of(part * half, half)
            span = pl.ds(first, half)
            total = dot(rows_hot(far_keys[u], first, half), values)
            total = total + far.got[t, span, :].astype(jnp.float32)

            @pl.when(t == ZN - 1)
            def _():
                last = far.got[ZN, span, :].astype(jnp.float32)
                across.src[span, :] = (total + last).astype(jnp.bfloat16)

            @pl.when(t < ZN - 1)
            def _():
                far.out[t, span, :] = total.astype(jnp.bfloat16)

        far.start(t)
        pl.when(t == ZN - 1)(across.start)

    def near_up(t):
        u = here.plane(sum_off(t))
        rows.arrived(u)
        near.hold(t)
        pl.when(t == ZN - 1)(across.arrived)

        @pl.loop(0, 2)
        def _(part):
            first = pl.multiple_of(part * half, half)
            span = pl.ds(first, half)
            total = dot(rows_hot(keys[u], first, half), rows.into[u])
            total = total + near.got[t, span, :].astype(jnp.float32)

            @pl.when(t == ZN - 1)
            def _():
                last = near.got[ZN, span, :].astype(jnp.float32)
                finish(span, total + last + across.dst[span, :].astype(jnp.float32))

            @pl.when(t < ZN - 1)
            def _():
                near.out[t, span, :] = total.astype(jnp.bfloat16)

        near.start(t)

    @pl.loop(0, ZN + 2)
    def _(i):
        @pl.when(i < ZN)
        def _():
            u = here.plane(sum_off(i))
            produce(i, u)
            rows.start(u)
            far_up(i, u)

        pl.when(i == ZN)(across.pass_on)
        pl.when(i >= 2)(lambda: near_up(i - 2))

    for part in (rows, near, far, across):
        part.close()


def cast_to_children(here, rows, near, far, across, keys, far_keys, prepare, consume):
    def chosen(wanted, chunk):
        places = turned(wanted).astype(jnp.int16)
        return dot(columns_hot(places, chunk.shape[0]), chunk).astype(jnp.bfloat16)

    @pl.loop(0, ZN + 2)
    def _(i):
        @pl.when(i < ZN)
        def _():
            near.step(i)
            pl.when(i == 0)(across.start)
            u = here.plane(cast_off(i))

            @pl.loop(0, 3)
            def _(j):
                span = block_at(lax.rem(here.x + 3 + j, XN), rows.block)
                rows.out[u, span, :] = chosen(keys[u, :, span], near.chunks[i])

            rows.start(u)

        pl.when(i == 1)(across.arrived)
        pl.when((i >= 1) & (i <= ZN))(lambda: far.step(i - 1))
        prepare(i)
        pl.when(i == 0)(across.pass_on)

        @pl.when(i >= 2)
        def _():
            u = here.plane(cast_off(i - 2))
            rows.into[u, block_at(here.far, rows.block), :] = chosen(far_keys[u], far.chunks[i - 2])
            rows.arrived(u)
            consume(i - 2, u)

    for part in (rows, near, far, across):
        part.close()


def to_slots(slots, values, first, count):
    nodes = values.shape[0]
    step = min(1024, nodes)
    total = jnp.zeros((count, values.shape[1]), jnp.float32)
    for at in range(0, nodes, step):
        total = total + dot(rows_hot(slots[:, at:at + step], first, count), values[at:at + step, :])
    return total.astype(jnp.bfloat16)


class Total:
    def __init__(self, here, part, scale, by_g, mid, by_x, one, by_z, done, full_x, full, sems):
        self.here, self.part, self.scale = here, part, scale
        self.by_g, self.mid, self.by_x, self.one = by_g, mid, by_x, one
        self.by_z, self.done, self.full_x, self.full = by_z, done, full_x, full
        self.sems = sems
        self.groups = part.shape[1]

    def peers(self, stage):
        here, groups = self.here, self.groups
        if stage in (0, 4):
            return [lax.rem(here.g + i, groups) for i in range(1, groups)]
        if stage == 2:
            return [here.plane(i) for i in range(1, ZN)]
        return [lax.rem(here.x + i, XN) for i in range(1, XN)]

    def copy(self, stage, i, peer):
        here = self.here
        send, recv = self.sems.at[0, stage, i], self.sems.at[1, stage, i]
        if stage == 0:
            return remote(self.part.at[:, peer], self.by_g.at[:, here.g], send, recv, {"grp": peer})
        if stage == 1:
            return remote(self.mid.at[:, peer], self.by_x.at[:, here.x], send, recv, here.at_x(peer))
        if stage == 2:
            return remote(self.one, self.by_z.at[here.z], send, recv, {"dev": peer * XN + here.x})
        if stage == 3:
            return remote(self.done, self.full_x.at[:, here.x], send, recv, here.at_x(peer))
        return remote(self.full_x, self.full.at[:, here.g], send, recv, {"grp": peer})

    def start(self, stage):
        here = self.here
        for i, peer in enumerate(self.peers(stage)):
            self.copy(stage, i, peer).start()
        if stage == 0:
            self.by_g[:, here.g] = self.part[:, here.g]
        elif stage == 1:
            self.by_x[:, here.x] = self.mid[:, here.x]
        elif stage == 2:
            self.by_z[here.z] = self.one[...]
        elif stage == 3:
            self.full_x[:, here.x] = self.done[...]
        else:
            self.full[:, here.g] = self.full_x[...]

    def end(self, stage):
        for i, peer in enumerate(self.peers(stage)):
            self.copy(stage, i, peer).wait()
        if stage == 0:
            self.mid[...] = jnp.sum(self.by_g[...], axis=1).reshape(self.mid.shape)
        elif stage == 1:
            self.one[...] = jnp.sum(self.by_x[...], axis=1)
        elif stage == 2:
            self.done[...] = jnp.sum(self.by_z[...], axis=0) * self.scale

    def next(self, stage):
        if stage:
            self.end(stage - 1)
        if stage < 5:
            self.start(stage)


def block_kernel(
    scale,
    feat, cot, slots, recv_row, coarse, wr, wc, wp,
    grad_node, grad_coarse, total_r, total_c, total_p,
    keys, far_keys, feat_slot, cot_slot, out, term,
    summed_b, update, places, grad_pre, back,
    into_a, into_b, near_out, near_got, far_out, far_got, near_chunks, far_chunks,
    far_sum, far_in, pass_ra, pass_la, pass_rb, pass_lb,
    x_send_a, x_recv_a, x_send_b, x_recv_b, f_send_a, f_recv_a, f_send_b, f_recv_b,
    zn_send_a, zn_recv_a, zn_send_b, zn_recv_b, zf_send_a, zf_recv_a, zf_send_b, zf_recv_b,
    k_send, k_recv, part_cp, part_r, *total_refs,
):
    here = Here()
    nodes = feat.shape[0]
    width = feat_slot.shape[1]
    count = width // 2
    step = min(512, nodes)
    groups = part_r.shape[1]
    kept = cot_slot.shape[0]
    block = width // XN

    near_sums = SumChain(here, near_out, near_got, zn_send_a, zn_recv_a)
    far_sums = SumChain(here, far_out, far_got, zf_send_a, zf_recv_a)
    far_back = Across(here, far_sum, far_in, pass_ra, pass_la, f_send_a, f_recv_a)
    near_cast = CastChain(here, near_chunks, zn_send_b, zn_recv_b)
    far_cast = CastChain(here, far_chunks, zf_send_b, zf_recv_b)
    far_over = Across(here, near_chunks.at[0], far_chunks.at[0], pass_rb, pass_lb, f_send_b, f_recv_b)
    near_sums.clear()
    far_sums.clear()
    into_a[:, block_at(here.far, block), :] = jnp.zeros((ZN, block, into_a.shape[2]), into_a.dtype)
    part_cp[...] = jnp.zeros_like(part_cp)
    part_r[...] = jnp.zeros_like(part_r)
    here.greet(groups)

    def key_copy(off):
        to = here.plane(off)
        return remote(
            recv_row.at[to], keys.at[here.z], k_send.at[off], k_recv.at[off], {"dev": to * XN + here.x}
        )

    def far_key_copy(off):
        to = here.plane(off)
        return remote(
            recv_row.at[to, :, block_at(here.far, block)],
            far_keys.at[here.z],
            k_send.at[ZN + off],
            k_recv.at[ZN + off],
            {"dev": to * XN + here.far},
        )

    key_copies = [functools.partial(far_key_copy, off) for off in range(ZN)]
    key_copies += [functools.partial(key_copy, off) for off in range(1, ZN)]
    for copy in key_copies:
        copy().start()
    keys[here.z] = recv_row[here.z]

    def add(ref, at, value):
        ref[at] += value.reshape(ref.shape[1:])

    def make_message(t, u):
        @pl.loop(0, 2)
        def _(part):
            span = pl.ds(pl.multiple_of(part * count, count), count)
            found = to_slots(slots, feat, u * width + part * count, count)
            feat_slot[u, span, :] = found
            pre = dot(found, wr[...])
            out[u, span, :] = (pre * jax.nn.sigmoid(pre)).astype(jnp.bfloat16)

        @pl.when(t == 0)
        def _():
            for copy in key_copies:
                copy().wait_recv()

    def coarse_update(span, total):
        summed = coarse[span, :].astype(jnp.float32) + total
        rounded = summed.astype(jnp.bfloat16)
        moved = dot(rounded, wc[...])
        summed_b[span, :] = rounded
        update[span, :] = moved
        near_chunks[0, span, :] = (summed + moved * jax.nn.sigmoid(moved)).astype(jnp.bfloat16)

    rows_a = Rows(here, out, into_a, x_send_a, x_recv_a)
    sum_to_owners(
        here, rows_a, near_sums, far_sums, far_back, make_message, keys, far_keys, coarse_update
    )
    for copy in key_copies:
        copy().wait_send()

    def place_cotangent(i):
        @pl.when(i < ZN)
        def _():
            first = here.plane(cast_off(i)) * width
            spot = lax.rem(i, kept)

            @pl.loop(0, 2)
            def _(part):
                span = pl.ds(pl.multiple_of(part * count, count), count)
                cot_slot[spot, span, :] = to_slots(slots, cot, first + part * count, count)

    def make_term(t, u):
        spot = lax.rem(t, kept)

        @pl.loop(0, 2)
        def _(part):
            span = pl.ds(pl.multiple_of(part * count, count), count)
            parent = into_b[u, span, :]
            proj = dot(parent, wp[...])
            grad = (cot_slot[spot, span, :].astype(jnp.float32) * dsilu(proj)).astype(jnp.bfloat16)
            add(part_cp, 1, left_dot(parent, grad))
            term[u, span, :] = right_dot(grad, wp[...]).astype(jnp.bfloat16)

    rows_b = Rows(here, out, into_b, x_send_b, x_recv_b)
    cast_to_children(
        here, rows_b, near_cast, far_cast, far_over, keys, far_keys, place_cotangent, make_term
    )

    def coarse_gradient(span, total):
        grad_update = (total * dsilu(update[span, :])).astype(jnp.bfloat16)
        grad = (total + right_dot(grad_update, wc[...])).astype(jnp.bfloat16)
        grad_coarse[span, :] = grad
        near_chunks[0, span, :] = grad
        add(part_cp, 0, left_dot(summed_b[span, :], grad_update))

    rows_a = Rows(here, term, into_a, x_send_a, x_recv_a)
    sum_to_owners(
        here, rows_a, near_sums, far_sums, far_back, lambda t, u: None, keys, far_keys, coarse_gradient
    )

    sums_cp = Total(here, part_cp, scale, *total_refs[:8], total_refs[16])
    sums_r = Total(here, part_r, scale, *total_refs[8:16], total_refs[17])

    def other_sums(i):
        for stage in range(6):
            pl.when(i == stage)(functools.partial(sums_cp.next, stage))

        @pl.when(i == 0)
        def _():
            back[...] = jnp.zeros_like(back)
            for at in range(0, nodes, step):
                places[at:at + step, :] = turned(slots[:, at:at + step])

    def node_gradient(t, u):
        @pl.loop(0, 2)
        def _(part):
            span = pl.ds(pl.multiple_of(part * count, count), count)
            found = feat_slot[u, span, :]
            pre = dot(found, wr[...])
            grad = (into_b[u, span, :].astype(jnp.float32) * dsilu(pre)).astype(jnp.bfloat16)
            add(part_r, 0, left_dot(found, grad))
            grad_pre[span, :] = grad

        pl.when(t == ZN - 1)(functools.partial(sums_r.next, 0))
        first = u * width

        @pl.loop(0, nodes // step)
        def _(part):
            span = pl.ds(pl.multiple_of(part * step, step), step)
            wanted = (places[span, :] - first).astype(jnp.int16)
            found = dot(columns_hot(wanted, width), grad_pre[...])
            back[span, :] = (back[span, :].astype(jnp.float32) + found).astype(jnp.bfloat16)

    cast_to_children(
        here, rows_b, near_cast, far_cast, far_over, keys, far_keys, other_sums, node_gradient
    )
    sums_r.next(1)

    @pl.loop(0, nodes // step)
    def _(part):
        span = pl.ds(pl.multiple_of(part * step, step), step)
        grad_node[span, :] = (
            cot[span, :].astype(jnp.float32) + right_dot(back[span, :], wr[...])
        ).astype(jnp.bfloat16)

    for stage in range(2, 6):
        sums_r.next(stage)
    total_r[...] = sums_r.full[0].reshape(total_r.shape)
    total_c[...] = sums_cp.full[0].reshape(total_c.shape)
    total_p[...] = sums_cp.full[1].reshape(total_p.shape)


def total_scratch(m, groups, width):
    rows = width // groups
    part = rows // XN
    return [
        pltpu.VMEM((m, groups, rows, width), jnp.float32),
        pltpu.VMEM((m, XN, part, width), jnp.float32),
        pltpu.VMEM((m, XN, part, width), jnp.float32),
        pltpu.VMEM((m, part, width), jnp.float32),
        pltpu.VMEM((ZN, m, part, width), jnp.float32),
        pltpu.VMEM((m, part, width), jnp.float32),
        pltpu.VMEM((m, XN, part, width), jnp.float32),
        pltpu.VMEM((m, groups, XN, part, width), jnp.float32),
    ]


def local(
    node_feat, coarse_feat, cotangent, w_restrict, w_coarse, w_prolong, owner, slot, recv_row
):
    devs = ZN * XN
    groups = lax.axis_size("grp")
    nodes, width = node_feat.shape
    coarse_rows = coarse_feat.shape[0]
    block = recv_row.shape[0] // devs
    plane_rows = XN * block
    bf, f32 = jnp.bfloat16, jnp.float32
    shape = jax.ShapeDtypeStruct
    dma = pltpu.SemaphoreType.DMA
    vmem = pltpu.VMEM
    wide = vmem((ZN, plane_rows, width), bf)
    chain = vmem((ZN, coarse_rows, width), bf)
    chain_in = vmem((ZN + 1, coarse_rows, width), bf)
    chunk = vmem((coarse_rows, width), bf)
    passing = vmem((coarse_rows // 2, width), bf)
    scratch = [
        vmem((ZN, 1, plane_rows), jnp.int32),
        vmem((ZN, 1, block), jnp.int32),
        wide,
        vmem((4, plane_rows, width), bf),
        wide,
        wide,
        chunk,
        vmem((coarse_rows, width), f32),
        vmem((nodes, 128), jnp.int32),
        vmem((plane_rows, width), bf),
        vmem((nodes, width), bf),
        wide, wide,
        chain, chain_in, chain, chain_in, chain, chain,
        chunk, chunk, passing, passing, passing, passing,
    ]
    scratch += [dma((2, ZN))] * 4 + [dma((4,))] * 4 + [dma((ZN,)), dma((ZN + 1,))] * 4
    scratch += [dma((2 * ZN,))] * 2
    scratch += [
        vmem((2, groups, width // groups, width), f32),
        vmem((1, groups, width // groups, width), f32),
    ]
    scratch += total_scratch(2, groups, width) + total_scratch(1, groups, width)
    scratch += [dma((2, 5, ZN))] * 2
    in_vmem = pl.BlockSpec(memory_space=pltpu.VMEM)
    scale = float(nodes * devs * groups) ** (-0.5)
    weight = shape((width, width), f32)
    return pl.pallas_call(
        functools.partial(block_kernel, scale),
        out_shape=(
            shape((nodes, width), bf),
            shape((coarse_rows, width), bf),
            weight, weight, weight,
        ),
        in_specs=[in_vmem] * 8,
        out_specs=(in_vmem,) * 5,
        scratch_shapes=scratch,
        compiler_params=pltpu.CompilerParams(
            collective_id=0, has_side_effects=True, vmem_limit_bytes=62 * 2**20
        ),
    )(
        node_feat, cotangent, (owner * block + slot).reshape(1, nodes),
        recv_row.reshape(ZN, 1, plane_rows), coarse_feat, w_restrict, w_coarse, w_prolong,
    )

def solution(mesh):
    return jax.shard_map(
        local,
        mesh=mesh,
        in_specs=(
            P(("grp", "dev"), None),
            P(("grp", "dev"), None),
            P(("grp", "dev"), None),
            P(),
            P(),
            P(),
            P(("grp", "dev")),
            P(("grp", "dev")),
            P(("grp", "dev")),
        ),
        out_specs=(P(("grp", "dev"), None), P(("grp", "dev"), None), P(), P(), P()),
        check_vma=False,
    )
```

time: 268 us -> 277 us (1.034)
  Pallas kernels: 260 us -> 268 us
    pallas_call x1, Pallas kernels: 260 us -> 268 us  [local(): pl.pallas_call(functools.partial(block_kernel, scale), out_shape=(shape((...]
    unnamed x4 -> x13, local copies, waits for them, and re-layouts: 3.79 us -> 5.95 us
where the time goes in v2:
time: 277 us; the launch traced here: 276 us
  Pallas kernels  268 us (97%)
  local copies, waits for them, and re-layouts  5.95 us (2%)
    pallas_call x1, Pallas kernels, local(): pl.pallas_call(functools.partial(block_kernel, scale), out_shape=(shape((...  268 us
    unnamed x13, local copies, waits for them, and re-layouts  5.95 us

profile of v2, /device:TPU:1, one launch (start us, length us, event | category | flops | bytes accessed | tf_op | source)
XLA Modules:
  0.0 276.3 jit_solution(11154062397041735003)
XLA Ops:
  0.6 1.3 multiply_add_fusion
  2.0 268.3 %shard_map.128 = (bf16[4096,256]{1,0:T(8,128)(2,1)}, bf16[512,256]{1,0:T(8,128)(2,1)}, f32[256,256]{1,0:T(8,128)}, f32[256,256]{1,0:T(8,128)}, f32[256,256]{1,0:T(8,128)}) custom-call(bf16[4096,256]{1,0:T(8,128)(2,1)} %feat.1, bf16[4096,256]{1,0:T(8,128)(2,1)} %cot.1, s32[1,4096]{1,0:T(1,128)} %bitcast.2, s32[8,1,1024]{2,1,0:T(1,128)} %bitcast.3, ...), custom_call_target="tpu_custom_call" | custom-call | tf_op jit(solution)/shard_map/pallas_call | solution.py:686
  270.3 0.0 copy-start.3
  270.3 0.0 copy-start.2
  270.4 0.0 copy-start.1
  270.4 0.0 copy-start
  270.4 3.1 %copy.19 = bf16[4096,256]{1,0:T(8,128)(2,1)} copy(bf16[4096,256]{1,0:T(8,128)(2,1)} %get-tuple-element.10) | data formatting | bytes 4194304
  273.5 0.0 copy-done.3
  273.5 0.7 copy.20
  274.2 0.0 copy-done.2
  274.2 0.7 copy.21
  274.9 0.0 copy-done.1
  274.9 0.7 copy.22
  275.6 0.0 copy-done
  275.6 0.7 copy.23
Async XLA Ops:
  270.3 3.2 %copy-start.3 = (bf16[512,256]{1,0:T(8,128)(2,1)S(1)}, bf16[512,256]{1,0:T(8,128)(2,1)}, u32[]{:S(2)}) copy-start(bf16[512,256]{1,0:T(8,128)(2,1)} %get-tuple-element.11) | copy-start | bytes 786436
  270.3 3.9 %copy-start.2 = (f32[256,256]{1,0:T(8,128)S(1)}, f32[256,256]{1,0:T(8,128)}, u32[]{:S(2)}) copy-start(f32[256,256]{1,0:T(8,128)} %get-tuple-element.12) | copy-start | bytes 786436
  270.4 4.6 %copy-start.1 = (f32[256,256]{1,0:T(8,128)S(1)}, f32[256,256]{1,0:T(8,128)}, u32[]{:S(2)}) copy-start(f32[256,256]{1,0:T(8,128)} %get-tuple-element.13) | copy-start | bytes 786436
  270.4 5.3 %copy-start = (f32[256,256]{1,0:T(8,128)S(1)}, f32[256,256]{1,0:T(8,128)}, u32[]{:S(2)}) copy-start(f32[256,256]{1,0:T(8,128)} %get-tuple-element.14) | copy-start | bytes 786436

commit v3 on v1

--- a/solution.py
+++ b/solution.py
@@ -38,15 +38,25 @@
 
 
 def rows_hot(keys, first, count):
-    shape = (count, keys.shape[1])
-    at = lax.broadcasted_iota(jnp.int32, shape, 0).astype(jnp.int16)
-    return hot(at == jnp.broadcast_to((keys - first).astype(jnp.int16), shape))
+    lanes = min(128, keys.shape[1])
+    at = lax.broadcasted_iota(jnp.int32, (count, lanes), 0).astype(jnp.int16)
+    wanted = (keys - first).astype(jnp.int16)
+    parts = [
+        hot(at == jnp.broadcast_to(wanted[:, lane:lane + lanes], at.shape))
+        for lane in range(0, keys.shape[1], lanes)
+    ]
+    return jnp.concatenate(parts, axis=1)
 
 
 def columns_hot(keys, count):
-    lanes = keys.shape[1]
-    at = lax.broadcasted_iota(jnp.int32, keys.shape, 1)
-    parts = [hot((at + lane).astype(jnp.int16) == keys) for lane in range(0, count, lanes)]
+    rows, lanes = keys.shape
+    tile = min(16, rows)
+    at = lax.broadcasted_iota(jnp.int32, (1, tile, lanes), 2)
+    tiled = keys.reshape(rows // tile, tile, lanes)
+    parts = [
+        hot(tiled == jnp.broadcast_to((at + lane).astype(jnp.int16), tiled.shape)).reshape(rows, lanes)
+        for lane in range(0, count, lanes)
+    ]
     return jnp.concatenate(parts, axis=1)
 
 
@@ -174,20 +184,22 @@
         pl.when(t >= 3)(lambda: z_copy(t - 2).wait_recv())
         pl.when(t == ZN - 1)(lambda: z_copy(t - 1).wait_recv())
 
-        @pl.loop(0, 2)
-        def _(part):
-            first = pl.multiple_of(part * half, half)
-            span = pl.ds(first, half)
-            total = dot(rows_hot(keys[u], first, half), rows.into[u])
-            total = total + got[t, span, :].astype(jnp.float32)
-
-            @pl.when(t == ZN - 1)
-            def _():
-                finish(span, total + got[ZN, span, :].astype(jnp.float32))
-
-            @pl.when(t < ZN - 1)
-            def _():
-                out_z[t, span, :] = total.astype(jnp.bfloat16)
+        def total(part):
+            span = pl.ds(part * half, half)
+            found = dot(rows_hot(keys[u], part * half, half), rows.into[u])
+            return span, found + got[t, span, :].astype(jnp.float32)
+
+        @pl.when(t == ZN - 1)
+        def _():
+            for part in range(2):
+                span, found = total(part)
+                finish(span, found + got[ZN, span, :].astype(jnp.float32))
+
+        @pl.when(t < ZN - 1)
+        def _():
+            for part in range(2):
+                span, found = total(part)
+                out_z[t, span, :] = found.astype(jnp.bfloat16)
 
         @pl.when(t == 0)
         def _():
@@ -223,7 +235,7 @@
         z_copy(t).wait_send()
 
 
-def cast_to_children(here, rows, keys, prepare, consume, chunks, z_send, z_recv):
+def cast_to_children(here, rows, places_of, prepare, consume, chunks, z_send, z_recv):
     half = chunks.shape[1] // 2
     low, high = pl.ds(0, half), pl.ds(half, half)
     count = rows.out.shape[1] // 2
@@ -264,12 +276,9 @@
             last_down().wait_recv()
             last_up().wait_recv()
 
-        wanted = keys[u]
         for part in range(2):
             span = pl.ds(part * count, count)
-            chosen = columns_hot(
-                turned(wanted[:, part * count:(part + 1) * count]).astype(jnp.int16), chunks.shape[1]
-            )
+            chosen = columns_hot(places_of(u, part * count, count), chunks.shape[1])
             rows.out[u, span, :] = dot(chosen, chunks[t]).astype(jnp.bfloat16)
 
     @pl.loop(0, ZN + 2)
@@ -374,9 +383,9 @@
 def block_kernel(
     scale,
     feat, cot, slots, recv_row, coarse, wr, wc, wp,
-    grad_node, grad_coarse, totals,
+    grad_node, grad_coarse, total_r, total_c, total_p,
     keys, feat_slot, cot_slot, out, term,
-    summed_b, update, places, grad_pre, back,
+    summed_b, update, key_places, places, grad_pre, back,
     into_a, pass_ra, pass_la, into_b, pass_rb, pass_lb, out_z, got, chunks,
     x_send_a, x_recv_a, x_send_b, x_recv_b, z_send_a, z_recv_a, z_send_b, z_recv_b, k_send, k_recv,
     part_cp, part_r, *total_refs,
@@ -388,7 +397,6 @@
     step = min(512, nodes)
     half = coarse.shape[0] // 2
     groups = part_r.shape[1]
-    kept = cot_slot.shape[0]
 
     got[0] = jnp.zeros_like(got[0])
     got[1, half:, :] = jnp.zeros_like(got[1, half:, :])
@@ -411,9 +419,8 @@
         ref[at] += value.reshape(ref.shape[1:])
 
     def make_message(t, u):
-        @pl.loop(0, 2)
-        def _(part):
-            span = pl.ds(pl.multiple_of(part * count, count), count)
+        for part in range(2):
+            span = pl.ds(part * count, count)
             block = to_slots(slots, feat, u * width + part * count, count)
             feat_slot[u, span, :] = block
             pre = dot(block, wr[...])
@@ -440,28 +447,38 @@
     def place_cotangent(i):
         @pl.when(i < ZN)
         def _():
-            first = here.plane(cast_off(i)) * width
-            spot = lax.rem(i, kept)
-
-            @pl.loop(0, 2)
-            def _(part):
-                span = pl.ds(pl.multiple_of(part * count, count), count)
-                cot_slot[spot, span, :] = to_slots(slots, cot, first + part * count, count)
+            u = here.plane(cast_off(i))
+            for part in range(2):
+                span = pl.ds(part * count, count)
+                cot_slot[u, span, :] = to_slots(slots, cot, u * width + part * count, count)
+
+    def new_places(u, first, count):
+        found = turned(keys[u, :, first:first + count]).astype(jnp.int16)
+        key_places[u, first:first + count, :] = found
+        return found
+
+    def old_places(u, first, count):
+        return key_places[u, first:first + count, :]
 
     def make_term(t, u):
-        spot = lax.rem(t, kept)
-
-        @pl.loop(0, 2)
-        def _(part):
-            span = pl.ds(pl.multiple_of(part * count, count), count)
+        for part in range(2):
+            span = pl.ds(part * count, count)
             parent = into_b[u, span, :]
             proj = dot(parent, wp[...])
-            grad = (cot_slot[spot, span, :].astype(jnp.float32) * dsilu(proj)).astype(jnp.bfloat16)
+            grad = (cot_slot[u, span, :].astype(jnp.float32) * dsilu(proj)).astype(jnp.bfloat16)
             add(part_cp, 1, left_dot(parent, grad))
             term[u, span, :] = right_dot(grad, wp[...]).astype(jnp.bfloat16)
 
+        @pl.when(t == 2)
+        def _():
+            back[...] = jnp.zeros_like(back)
+            for at in range(0, nodes, step):
+                places[at:at + step, :] = turned(slots[:, at:at + step]).astype(jnp.int16)
+
     rows_b = Rows(here, out, into_b, pass_rb, pass_lb, x_send_b, x_recv_b)
-    cast_to_children(here, rows_b, keys, place_cotangent, make_term, chunks, z_send_b, z_recv_b)
+    cast_to_children(
+        here, rows_b, new_places, place_cotangent, lambda t, u: None, chunks, z_send_b, z_recv_b
+    )
 
     def coarse_gradient(span, total):
         grad_update = (total * dsilu(update[span, :])).astype(jnp.bfloat16)
@@ -472,7 +489,7 @@
 
     rows_a = Rows(here, term, into_a, pass_ra, pass_la, x_send_a, x_recv_a)
     sum_to_owners(
-        here, rows_a, lambda t, u: None, keys, coarse_gradient, out_z, got, z_send_a, z_recv_a
+        here, rows_a, make_term, keys, coarse_gradient, out_z, got, z_send_a, z_recv_a
     )
 
     sums_cp = Total(here, part_cp, scale, *total_refs[:8], total_refs[16])
@@ -482,16 +499,9 @@
         for stage in range(6):
             pl.when(i == stage)(functools.partial(sums_cp.next, stage))
 
-        @pl.when(i == 0)
-        def _():
-            back[...] = jnp.zeros_like(back)
-            for at in range(0, nodes, step):
-                places[at:at + step, :] = turned(slots[:, at:at + step])
-
     def node_gradient(t, u):
-        @pl.loop(0, 2)
-        def _(part):
-            span = pl.ds(pl.multiple_of(part * count, count), count)
+        for part in range(2):
+            span = pl.ds(part * count, count)
             block = feat_slot[u, span, :]
             pre = dot(block, wr[...])
             grad = (into_b[u, span, :].astype(jnp.float32) * dsilu(pre)).astype(jnp.bfloat16)
@@ -499,17 +509,17 @@
             grad_pre[span, :] = grad
 
         pl.when(t == ZN - 1)(functools.partial(sums_r.next, 0))
-        first = u * width
-
-        @pl.loop(0, nodes // step)
+        first = jnp.full((step, places.shape[1]), u * width, jnp.int32).astype(jnp.int16)
+
+        @pl.loop(0, nodes // step, unroll=2)
         def _(part):
             span = pl.ds(pl.multiple_of(part * step, step), step)
-            wanted = (places[span, :] - first).astype(jnp.int16)
+            wanted = places[span, :] - first
             found = dot(columns_hot(wanted, width), grad_pre[...])
             back[span, :] = (back[span, :].astype(jnp.float32) + found).astype(jnp.bfloat16)
 
     rows_b = Rows(here, out, into_b, pass_rb, pass_lb, x_send_b, x_recv_b)
-    cast_to_children(here, rows_b, keys, other_sums, node_gradient, chunks, z_send_b, z_recv_b)
+    cast_to_children(here, rows_b, old_places, other_sums, node_gradient, chunks, z_send_b, z_recv_b)
     sums_r.next(1)
 
     @pl.loop(0, nodes // step)
@@ -521,9 +531,9 @@
 
     for stage in range(2, 6):
         sums_r.next(stage)
-    totals[0] = sums_r.full[0].reshape(totals.shape[1:])
-    for at in (0, 1):
-        totals[at + 1] = sums_cp.full[at].reshape(totals.shape[1:])
+    total_r[...] = sums_r.full[0].reshape(total_r.shape)
+    total_c[...] = sums_cp.full[0].reshape(total_c.shape)
+    total_p[...] = sums_cp.full[1].reshape(total_p.shape)
 
 
 def total_scratch(m, groups, width):
@@ -559,12 +569,13 @@
     scratch = [
         vmem((ZN, 1, plane_rows), jnp.int32),
         wide,
-        vmem((4, plane_rows, width), bf),
+        wide,
         wide,
         wide,
         vmem((coarse_rows, width), bf),
         vmem((coarse_rows, width), f32),
-        vmem((nodes, 128), jnp.int32),
+        vmem((ZN, plane_rows, 128), jnp.int16),
+        vmem((nodes, 128), jnp.int16),
         vmem((plane_rows, width), bf),
         vmem((nodes, width), bf),
         wide, passing, passing,
@@ -582,15 +593,16 @@
     scratch += [dma((2, 5, ZN))] * 2
     in_vmem = pl.BlockSpec(memory_space=pltpu.VMEM)
     scale = float(nodes * devs * groups) ** (-0.5)
-    grad_node, grad_coarse, totals = pl.pallas_call(
+    weight = shape((width, width), f32)
+    return pl.pallas_call(
         functools.partial(block_kernel, scale),
         out_shape=(
             shape((nodes, width), bf),
             shape((coarse_rows, width), bf),
-            shape((3, width, width), f32),
+            weight, weight, weight,
         ),
         in_specs=[in_vmem] * 8,
-        out_specs=(in_vmem,) * 3,
+        out_specs=(in_vmem,) * 5,
         scratch_shapes=scratch,
         compiler_params=pltpu.CompilerParams(
             collective_id=0, has_side_effects=True, vmem_limit_bytes=62 * 2**20
@@ -599,8 +611,6 @@
         node_feat, cotangent, (owner * block + slot).reshape(1, nodes),
         recv_row.reshape(ZN, 1, plane_rows), coarse_feat, w_restrict, w_coarse, w_prolong,
     )
-    return grad_node, grad_coarse, totals[0], totals[1], totals[2]
-
 
 def solution(mesh):
     return jax.shard_map(

time: 268 us -> 269 us (level)
    unnamed x4 -> x13, local copies, waits for them, and re-layouts: 3.79 us -> 5.95 us
where the time goes in v3:
time: 269 us
  Pallas kernels  261 us (97%)
  local copies, waits for them, and re-layouts  5.95 us (2%)
    pallas_call x1, Pallas kernels, local(): pl.pallas_call(functools.partial(block_kernel, scale), out_shape=(shape((...  261 us
    unnamed x13, local copies, waits for them, and re-layouts  5.95 us

profile of v3, /device:TPU:1, one launch (start us, length us, event | category | flops | bytes accessed | tf_op | source)
XLA Modules:
  0.0 268.6 jit_solution(2477048132003687921)
XLA Ops:
  0.6 1.3 multiply_add_fusion
  2.0 260.7 %shard_map.128 = (bf16[4096,256]{1,0:T(8,128)(2,1)}, bf16[512,256]{1,0:T(8,128)(2,1)}, f32[256,256]{1,0:T(8,128)}, f32[256,256]{1,0:T(8,128)}, f32[256,256]{1,0:T(8,128)}) custom-call(bf16[4096,256]{1,0:T(8,128)(2,1)} %feat.1, bf16[4096,256]{1,0:T(8,128)(2,1)} %cot.1, s32[1,4096]{1,0:T(1,128)} %bitcast.2, s32[8,1,1024]{2,1,0:T(1,128)} %bitcast.3, ...), custom_call_target="tpu_custom_call" | custom-call | tf_op jit(solution)/shard_map/pallas_call | solution.py:597
  262.6 0.0 copy-start.3
  262.7 0.0 copy-start.2
  262.7 0.0 copy-start.1
  262.7 0.0 copy-start
  262.7 3.1 %copy.19 = bf16[4096,256]{1,0:T(8,128)(2,1)} copy(bf16[4096,256]{1,0:T(8,128)(2,1)} %get-tuple-element.10) | data formatting | bytes 4194304
  265.8 0.0 copy-done.3
  265.8 0.7 copy.20
  266.5 0.0 copy-done.2
  266.5 0.7 copy.21
  267.2 0.0 copy-done.1
  267.2 0.7 copy.22
  267.9 0.0 copy-done
  267.9 0.7 copy.23
Async XLA Ops:
  262.6 3.2 %copy-start.3 = (bf16[512,256]{1,0:T(8,128)(2,1)S(1)}, bf16[512,256]{1,0:T(8,128)(2,1)}, u32[]{:S(2)}) copy-start(bf16[512,256]{1,0:T(8,128)(2,1)} %get-tuple-element.11) | copy-start | bytes 786436
  262.7 3.9 %copy-start.2 = (f32[256,256]{1,0:T(8,128)S(1)}, f32[256,256]{1,0:T(8,128)}, u32[]{:S(2)}) copy-start(f32[256,256]{1,0:T(8,128)} %get-tuple-element.12) | copy-start | bytes 786436
  262.7 4.6 %copy-start.1 = (f32[256,256]{1,0:T(8,128)S(1)}, f32[256,256]{1,0:T(8,128)}, u32[]{:S(2)}) copy-start(f32[256,256]{1,0:T(8,128)} %get-tuple-element.13) | copy-start | bytes 786436
  262.7 5.3 %copy-start = (f32[256,256]{1,0:T(8,128)S(1)}, f32[256,256]{1,0:T(8,128)}, u32[]{:S(2)}) copy-start(f32[256,256]{1,0:T(8,128)} %get-tuple-element.14) | copy-start | bytes 786436

commit v4 on v3

--- a/solution.py
+++ b/solution.py
@@ -216,11 +216,14 @@
         def _():
             u = here.plane(sum_off(i))
             produce(i, u)
-            rows.start(u)
 
         @pl.when((i >= 1) & (i <= ZN))
         def _():
             rows.pass_on(here.plane(sum_off(i - 1)))
+
+        @pl.when(i < ZN)
+        def _():
+            rows.start(here.plane(sum_off(i)))
 
         @pl.when(i >= 2)
         def _():
@@ -287,11 +290,14 @@
         def _():
             u = here.plane(cast_off(i))
             spread(i, u)
-            rows.start(u)
 
         @pl.when((i >= 1) & (i <= ZN))
         def _():
             rows.pass_on(here.plane(cast_off(i - 1)))
+
+        @pl.when(i < ZN)
+        def _():
+            rows.start(here.plane(cast_off(i)))
 
         prepare(i)
 

time: 269 us -> 261 us (0.970)
  Pallas kernels: 261 us -> 253 us
    pallas_call x1, Pallas kernels: 261 us -> 253 us  [local(): pl.pallas_call(functools.partial(block_kernel, scale), out_shape=(shape((...]
where the time goes in v4:
time: 261 us
  Pallas kernels  253 us (97%)
  local copies, waits for them, and re-layouts  5.95 us (2%)
    pallas_call x1, Pallas kernels, local(): pl.pallas_call(functools.partial(block_kernel, scale), out_shape=(shape((...  253 us
    unnamed x13, local copies, waits for them, and re-layouts  5.95 us

profile of v4, /device:TPU:1, one launch (start us, length us, event | category | flops | bytes accessed | tf_op | source)
XLA Modules:
  0.0 261.0 jit_solution(7591473651620414109)
XLA Ops:
  0.6 1.3 multiply_add_fusion
  2.0 253.0 %shard_map.128 = (bf16[4096,256]{1,0:T(8,128)(2,1)}, bf16[512,256]{1,0:T(8,128)(2,1)}, f32[256,256]{1,0:T(8,128)}, f32[256,256]{1,0:T(8,128)}, f32[256,256]{1,0:T(8,128)}) custom-call(bf16[4096,256]{1,0:T(8,128)(2,1)} %feat.1, bf16[4096,256]{1,0:T(8,128)(2,1)} %cot.1, s32[1,4096]{1,0:T(1,128)} %bitcast.2, s32[8,1,1024]{2,1,0:T(1,128)} %bitcast.3, ...), custom_call_target="tpu_custom_call" | custom-call | tf_op jit(solution)/shard_map/pallas_call | solution.py:603
  255.0 0.0 copy-start.3
  255.0 0.0 copy-start.2
  255.0 0.0 copy-start.1
  255.0 0.0 copy-start
  255.0 3.1 %copy.19 = bf16[4096,256]{1,0:T(8,128)(2,1)} copy(bf16[4096,256]{1,0:T(8,128)(2,1)} %get-tuple-element.10) | data formatting | bytes 4194304
  258.1 0.0 copy-done.3
  258.1 0.7 copy.20
  258.8 0.0 copy-done.2
  258.8 0.7 copy.21
  259.5 0.0 copy-done.1
  259.5 0.7 copy.22
  260.2 0.0 copy-done
  260.3 0.7 copy.23
Async XLA Ops:
  255.0 3.2 %copy-start.3 = (bf16[512,256]{1,0:T(8,128)(2,1)S(1)}, bf16[512,256]{1,0:T(8,128)(2,1)}, u32[]{:S(2)}) copy-start(bf16[512,256]{1,0:T(8,128)(2,1)} %get-tuple-element.11) | copy-start | bytes 786436
  255.0 3.9 %copy-start.2 = (f32[256,256]{1,0:T(8,128)S(1)}, f32[256,256]{1,0:T(8,128)}, u32[]{:S(2)}) copy-start(f32[256,256]{1,0:T(8,128)} %get-tuple-element.12) | copy-start | bytes 786436
  255.0 4.6 %copy-start.1 = (f32[256,256]{1,0:T(8,128)S(1)}, f32[256,256]{1,0:T(8,128)}, u32[]{:S(2)}) copy-start(f32[256,256]{1,0:T(8,128)} %get-tuple-element.13) | copy-start | bytes 786436
  255.0 5.3 %copy-start = (f32[256,256]{1,0:T(8,128)S(1)}, f32[256,256]{1,0:T(8,128)}, u32[]{:S(2)}) copy-start(f32[256,256]{1,0:T(8,128)} %get-tuple-element.14) | copy-start | bytes 786436
